TPU v7x, 32 devices: a whole 2x2x4 slice. The times are simulated.
32 devices in a mesh: groups: 2 (over y), dp: 4 (over z), expert: 2 (over x), mp: 2 (over core).
Axes of the slice: x: 2, y: 2, z: 4, core: 2. Of those that a mesh axis runs over, the one named last changes fastest.
Arguments:
- activations: bfloat16 [96, 6144], P(('groups', 'dp', 'expert')), parts along dimension 0, may hold values from -16 to 16
- gradients: bfloat16 [96, 8192], P(('groups', 'dp', 'expert'), 'mp'), parts along dimension 0, may hold values from -16 to 16
- expert_ids: int32 [96, 1], P(('groups', 'dp', 'expert')), parts along dimension 0, may hold values from 0 to 1; in each aligned block of 6 rows (0 to 5, 6 to 11, ...) at most 5 rows name the same one
- example_ids: int32 [96], P(('groups', 'dp', 'expert')), parts along dimension 0, may hold values from 0 to 31
- example_slots: int32 [64], P('groups'), parts along dimension 0, may hold values from 0 to 31, each once
- eigenbasis: bfloat16 [2, 6144, 6144], P('expert', None, ('dp', 'mp')), may hold values from -0.078125 to 0.078125
- input_eigen: float32 [2, 6144], P('expert', ('dp', 'mp')), may hold values from 0.05 to 5
- output_eigen: float32 [2, 8192], P('expert', 'mp'), may hold values from 0.05 to 5
Outputs:
- influence: float32 [64, 32], P(('groups', 'dp', 'expert')), parts along dimension 0
There are 2 independent parts, one for each index of `groups`. A program takes and returns all parts, laid end to end along the dimension named above; an argument that names none is the same for every part. Nothing has to cross between parts.
Inputs may be any that keep to these rules, and one draw needn't show every extreme that they name: `expert_ids`: within the rows of one source device (aligned blocks of 6 rows) no expert is named by more than 5 rows, and in every draw some expert is named by exactly 5 rows of some block.
All inputs are finite; a program needn't handle non-finite values.
Results may differ from a plain program's by a relative error of at most 0.0003.
Values may be sent and summed in bfloat16 or wider, within the bound.
A program may use at most 128 MiB of HBM per device.

v0:
```python
import jax
import jax.numpy as jnp
from jax import lax
from jax.sharding import PartitionSpec as P

D = 6144
FF = 8192
CAP = 5


eigen_floor = 0.01
ridge_term = 500.0


def shifted(x, axis, by):
    size = lax.axis_size(axis)
    return lax.ppermute(x, axis, [(i, (i + by) % size) for i in range(size)])


def member_table(slot_list, example_count):
    return (slot_list[:, None] == jnp.arange(example_count, dtype=jnp.int32)[None, :]).astype(
        jnp.float32
    )


def solve_system(system_rows, first_row):
    order = system_rows.shape[0]
    square = lax.dynamic_slice_in_dim(system_rows, first_row, order, 1)
    square = square + ridge_term * jnp.eye(order, dtype=system_rows.dtype)
    factor = jnp.linalg.cholesky(square)
    middle = lax.linalg.triangular_solve(factor, system_rows, left_side=True, lower=True)
    return lax.linalg.triangular_solve(factor, middle, left_side=True, lower=True, transpose_a=True)


def on_device(
    activations,
    gradients,
    expert_ids,
    example_ids,
    example_slots,
    eigenbasis,
    input_eigen,
    output_eigen,
):
    data_ways = lax.axis_size("dp")
    expert_ways = lax.axis_size("expert")
    example_count = example_slots.shape[0]
    slot_width = expert_ways * CAP
    chosen = expert_ids[:, 0]
    onehot = (chosen[:, None] == jnp.arange(expert_ways, dtype=jnp.int32)[None, :]).astype(
        jnp.int32
    )
    position = jnp.sum((jnp.cumsum(onehot, axis=0) - onehot) * onehot, axis=1)
    target = chosen * CAP + position
    placing = target[None, :] == jnp.arange(slot_width, dtype=jnp.int32)[:, None]
    placing_table = placing.astype(jnp.bfloat16)
    lookup = (example_ids[:, None] == jnp.arange(example_count, dtype=jnp.int32)[None, :]).astype(
        jnp.int32
    )
    row_slot = jnp.sum(lookup * example_slots[None, :], axis=1)
    send_inputs = jnp.dot(placing_table, activations, preferred_element_type=jnp.float32).astype(
        jnp.bfloat16
    )
    send_grads = jnp.dot(placing_table, gradients, preferred_element_type=jnp.float32).astype(
        jnp.bfloat16
    )
    send_slots = jnp.sum(jnp.where(placing, row_slot[None, :] + 1, 0), axis=1) - 1
    got_inputs, got_grads, got_slots = (
        lax.all_to_all(
            send_inputs.reshape(expert_ways, CAP, -1),
            "expert",
            split_axis=0,
            concat_axis=0,
            tiled=True,
        ),
        lax.all_to_all(
            send_grads.reshape(expert_ways, CAP, -1),
            "expert",
            split_axis=0,
            concat_axis=0,
            tiled=True,
        ),
        lax.all_to_all(
            send_slots.reshape(expert_ways, CAP), "expert", split_axis=0, concat_axis=0, tiled=True
        ),
    )
    own_inputs = got_inputs.reshape(slot_width, -1)
    own_grads = got_grads.reshape(slot_width, -1)
    own_slots = got_slots.reshape(slot_width)
    basis_block = eigenbasis[0]
    scale_in = lax.rsqrt(input_eigen[0] + eigen_floor)
    rotated = (
        jnp.dot(
            lax.all_gather(own_inputs, "dp", axis=0, tiled=True),
            basis_block,
            preferred_element_type=jnp.float32,
        )
        * scale_in
    ).astype(jnp.bfloat16)
    gram_part = (
        lax.dot_general(
            rotated, rotated, (((1,), (1,)), ((), ())), preferred_element_type=jnp.float32
        )
        / D
    )
    dp_index = lax.axis_index("dp")
    gram_in = lax.psum(gram_part, ("dp", "mp"))
    own_gram = lax.dynamic_slice_in_dim(gram_in, dp_index * slot_width, slot_width, 0)
    scaled = (own_grads.astype(jnp.float32) * lax.rsqrt(output_eigen[0] + eigen_floor)).astype(
        jnp.bfloat16
    )
    own_members = member_table(own_slots, example_count)

    def pair_terms(peer_grads, peer_slots, first_row):
        gram_out = (
            lax.dot_general(
                scaled, peer_grads, (((1,), (1,)), ((), ())), preferred_element_type=jnp.float32
            )
            / FF
        )
        weights = lax.dynamic_slice_in_dim(own_gram, first_row, peer_grads.shape[0], 1) * gram_out
        return jnp.dot(
            weights, member_table(peer_slots, example_count), precision=lax.Precision.HIGHEST
        )

    one_way = pair_terms(scaled, own_slots, dp_index * slot_width)
    both_ways = jnp.zeros_like(one_way)
    for offset in range(1, data_ways // 2 + 1):
        peer_grads, peer_slots = shifted((scaled, own_slots), "dp", offset)
        source_index = (dp_index - offset) % data_ways
        contribution = pair_terms(peer_grads, peer_slots, source_index * slot_width)
        if 2 * offset < data_ways:
            both_ways = both_ways + contribution
        else:
            one_way = one_way + contribution
    kernel = lax.dot_general(
        own_members, one_way + both_ways, (((0,), (0,)), ((), ())), precision=lax.Precision.HIGHEST
    )
    mirrored = lax.dot_general(
        own_members, both_ways, (((0,), (0,)), ((), ())), precision=lax.Precision.HIGHEST
    )
    kernel = kernel + mirrored.T
    shares = lax.psum_scatter(kernel, ("dp", "expert", "mp"), scatter_dimension=0, tiled=True)
    system_rows = lax.all_gather(shares, "mp", axis=0, tiled=True)
    first_row = (dp_index * expert_ways + lax.axis_index("expert")) * system_rows.shape[0]
    return solve_system(system_rows, first_row)


def solution(mesh):
    placed = (
        P(("groups", "dp", "expert"), None),
        P(("groups", "dp", "expert"), "mp"),
        P(("groups", "dp", "expert"), None),
        P(("groups", "dp", "expert")),
        P("groups"),
        P("expert", None, ("dp", "mp")),
        P("expert", ("dp", "mp")),
        P("expert", "mp"),
    )
    return jax.shard_map(
        on_device,
        mesh=mesh,
        in_specs=placed,
        out_specs=P(("groups", "dp", "expert"), None),
        check_vma=False,
    )
```

profile of v0, /device:TPU:0, one launch (start us, length us, event | category | flops | bytes accessed | tf_op | source)
XLA Modules:
  0.0 152.4 jit_solution(12051391119446637144)
XLA Ops:
  0.0 0.7 fusion.34
  0.9 0.7 select_reduce_fusion.3
  1.6 0.9 select_reduce_fusion.1
  2.4 0.7 multiply_add_fusion
  3.2 0.6 sub.16
  3.8 4.2 %all-to-all-start = ((s32[2,1,5]{2,1,0:T(1,128)}), s32[2,1,5]{2,1,0:T(1,128)S(1)}, u32[]{:S(2)}, u32[]{:S(2)}) async-start(s32[2,1,5]{2,1,0:T(1,128)} %bitcast.1), calls=%async_computation | async-start | bytes 2048 | tf_op jit(solution)/shard_map/all_to_all | solution.py:83
  8.0 1.1 convolution_convert_fusion.1
  9.2 0.7 reshape.73
  9.8 0.7 add_rsqrt_fusion
  10.6 0.3 convolution_convert_fusion
  10.9 0.8 all-to-all-done
  11.7 3.4 %all-to-all-start.2 = ((bf16[2,5,4096]{2,1,0:T(8,128)(2,1)}), bf16[2,5,4096]{2,1,0:T(8,128)(2,1)S(1)}, u32[]{:S(2)}, u32[]{:S(2)}) async-start(bf16[2,5,4096]{2,1,0:T(8,128)(2,1)} %reshape.73), calls=%async_computation.2 | async-start | bytes 262144 | tf_op jit(solution)/shard_map/all_to_all | solution.py:76
  15.1 0.7 rsqrt_reduce_fusion
  15.8 0.7 reshape.71
  16.6 1.2 dynamic-slice
  18.5 0.5 broadcast.155
  19.0 0.7 reduce.11
  19.7 2.0 %collective-permute-start.3 = (s32[10]{0:T(128)S(1)}, s32[10]{0:T(128)S(1)}, u32[]{:S(2)}, u32[]{:S(2)}) collective-permute-start(s32[10]{0:T(128)S(1)} %eq.50), channel_id=1, source_target_pairs={{0,4},{4,8},{8,12},{12,0},{1,5},{5,9},{9,13},{13,1},{2,6},{6,10},{... | collective-permute-start | bytes 128 | tf_op jit(solution)/shard_map/ppermute | solution.py:17
  21.7 2.6 %collective-permute-start.1 = (s32[10]{0:T(128)S(1)}, s32[10]{0:T(128)S(1)}, u32[]{:S(2)}, u32[]{:S(2)}) collective-permute-start(s32[10]{0:T(128)S(1)} %eq.50), channel_id=1, source_target_pairs={{0,8},{4,12},{8,0},{12,4},{1,9},{5,13},{9,1},{13,5},{2,10},{6,14},... | collective-permute-start | bytes 128 | tf_op jit(solution)/shard_map/ppermute | solution.py:17
  24.3 3.4 %all-to-all-start.1 = ((bf16[2,5,6144]{2,1,0:T(8,128)(2,1)}), bf16[2,5,6144]{2,1,0:T(8,128)(2,1)S(1)}, u32[]{:S(2)}, u32[]{:S(2)}) async-start(bf16[2,5,6144]{2,1,0:T(8,128)(2,1)} %reshape.71), calls=%async_computation.1 | async-start | bytes 393216 | tf_op jit(solution)/shard_map/all_to_all | solution.py:69
  27.9 1.9 %collective-permute-start = (bf16[10,4096]{1,0:T(8,128)(2,1)S(1)}, bf16[10,4096]{1,0:T(8,128)(2,1)S(1)}, u32[]{:S(2)}, u32[]{:S(2)}) collective-permute-start(bf16[10,4096]{1,0:T(8,128)(2,1)S(1)} %multiply_convert_fusion), channel_id=1, source_target_pairs={{0,8},{4,12},{8,0},{12,4},{1,9},{5,13},{9,1},{13,5},{2,10},{6,14},... | collective-permute-start | bytes 245768 | tf_op jit(solution)/shard_map/ppermute | solution.py:17
  29.9 2.7 %all-to-all-done.1 = bf16[2,5,6144]{2,1,0:T(8,128)(2,1)S(1)} async-done(((bf16[2,5,6144]{2,1,0:T(8,128)(2,1)}), bf16[2,5,6144]{2,1,0:T(8,128)(2,1)S(1)}, u32[]{:S(2)}, u32[]{:S(2)}) %all-to-all-start.1) | async-done | bytes 122912 | tf_op jit(solution)/shard_map/all_to_all | solution.py:69
  32.6 19.2 %all-gather = bf16[4,10,6144]{2,1,0:T(8,128)(2,1)S(1)} all-gather(bf16[1,10,6144]{2,1,0:T(8,128)(2,1)S(1)} %reshape.75), channel_id=1, replica_groups=mesh['groups'=2,'dp'=4,'expert'=2,'mp'=2] {'dp'}, dimensions={0}, use_global_device_ids=true | all-gather | bytes 614400 | tf_op jit(solution)/shard_map/all_gather | solution.py:94
  52.0 9.4 %fusion.11 = f32[40,40]{1,0:T(8,128)S(1)} fusion(bf16[40,6144]{1,0:T(8,128)(2,1)S(1)} %reshape.76, bf16[1,6144,768]{2,1,0:T(8,128)(2,1)} %param.13, f32[768]{0:T(1024)S(1)} %rsqrt_reduce_fusion), kind=kOutput, calls=%fused_computation.8 | convolution fusion | flops 380008000 | bytes 9938176 | tf_op jit(solution)/shard_map/dot_general | solution.py:101
  61.4 25.9 %psum.7 = f32[40,40]{1,0:T(8,128)S(1)} all-reduce(f32[40,40]{1,0:T(8,128)S(1)} %fusion.11), channel_id=1, replica_groups=mesh['groups'=2,'dp'=4,'expert'=2,'mp'=2] {'dp','mp'}, use_global_device_ids=true, to_apply=%region_4.5 | all-reduce | flops 1600 | bytes 12800 | tf_op jit(solution)/shard_map/psum | solution.py:107
  89.0 58.1 %all-reduce = f32[32,32]{1,0:T(8,128)S(1)} all-reduce(f32[32,32]{1,0:T(8,128)S(1)} %convolution_add_fusion), channel_id=2, replica_groups=mesh['groups'=2,'dp'=4,'expert'=2,'mp'=2] {'dp','expert','mp'}, use_global_device_ids=true, to_apply=%region_5.6.clone | all-reduce | flops 1024 | bytes 8192
  147.1 1.8 %all-gather.1 = f32[2,2,32]{2,1,0:T(2,128)S(1)} all-gather(f32[1,2,32]{2,1,0:T(2,128)S(1)} %dynamic-slice_bitcast_fusion), channel_id=1, replica_groups=mesh['groups'=2,'dp'=4,'expert'=2,'mp'=2] {'mp'}, dimensions={0}, use_global_device_ids=true | all-gather | bytes 768 | tf_op jit(solution)/shard_map/all_gather | solution.py:144
  149.2 0.4 cholesky.16
  149.7 0.6 compare_reduce_fusion
  150.4 0.6 select_select_fusion
  151.1 0.3 custom-call.8
  151.7 0.7 fusion.29
  (36 shorter events, 3.3 us)
Async XLA Ops:
  0.0 10.6 %copy-start = (bf16[6,6144]{1,0:T(8,128)(2,1)S(1)}, bf16[6,6144]{1,0:T(8,128)(2,1)}, u32[]{:S(2)}) copy-start(bf16[6,6144]{1,0:T(8,128)(2,1)} %param.8) | copy-start | bytes 221188
  3.8 7.9 %all-to-all-start = ((s32[2,1,5]{2,1,0:T(1,128)}), s32[2,1,5]{2,1,0:T(1,128)S(1)}, u32[]{:S(2)}, u32[]{:S(2)}) async-start(s32[2,1,5]{2,1,0:T(1,128)} %bitcast.1), calls=%async_computation | async-start | bytes 2048 | tf_op jit(solution)/shard_map/all_to_all | solution.py:83
  11.7 12.6 %all-to-all-start.2 = ((bf16[2,5,4096]{2,1,0:T(8,128)(2,1)}), bf16[2,5,4096]{2,1,0:T(8,128)(2,1)S(1)}, u32[]{:S(2)}, u32[]{:S(2)}) async-start(bf16[2,5,4096]{2,1,0:T(8,128)(2,1)} %reshape.73), calls=%async_computation.2 | async-start | bytes 262144 | tf_op jit(solution)/shard_map/all_to_all | solution.py:76
  19.7 68.2 %collective-permute-start.3 = (s32[10]{0:T(128)S(1)}, s32[10]{0:T(128)S(1)}, u32[]{:S(2)}, u32[]{:S(2)}) collective-permute-start(s32[10]{0:T(128)S(1)} %eq.50), channel_id=1, source_target_pairs={{0,4},{4,8},{8,12},{12,0},{1,5},{5,9},{9,13},{13,1},{2,6},{6,10},{... | collective-permute-start | bytes 128 | tf_op jit(solution)/shard_map/ppermute | solution.py:17
  21.7 66.5 %collective-permute-start.1 = (s32[10]{0:T(128)S(1)}, s32[10]{0:T(128)S(1)}, u32[]{:S(2)}, u32[]{:S(2)}) collective-permute-start(s32[10]{0:T(128)S(1)} %eq.50), channel_id=1, source_target_pairs={{0,8},{4,12},{8,0},{12,4},{1,9},{5,13},{9,1},{13,5},{2,10},{6,14},... | collective-permute-start | bytes 128 | tf_op jit(solution)/shard_map/ppermute | solution.py:17
  24.3 8.2 %all-to-all-start.1 = ((bf16[2,5,6144]{2,1,0:T(8,128)(2,1)}), bf16[2,5,6144]{2,1,0:T(8,128)(2,1)S(1)}, u32[]{:S(2)}, u32[]{:S(2)}) async-start(bf16[2,5,6144]{2,1,0:T(8,128)(2,1)} %reshape.71), calls=%async_computation.1 | async-start | bytes 393216 | tf_op jit(solution)/shard_map/all_to_all | solution.py:69
  27.8 59.9 %collective-permute-start.2 = (bf16[10,4096]{1,0:T(8,128)(2,1)S(1)}, bf16[10,4096]{1,0:T(8,128)(2,1)S(1)}, u32[]{:S(2)}, u32[]{:S(2)}) collective-permute-start(bf16[10,4096]{1,0:T(8,128)(2,1)S(1)} %multiply_convert_fusion), channel_id=1, source_target_pairs={{0,4},{4,8},{8,12},{12,0},{1,5},{5,9},{9,13},{13,1},{2,6},{6,10},{... | collective-permute-start | bytes 245768 | tf_op jit(solution)/shard_map/ppermute | solution.py:17
  27.9 60.2 %collective-permute-start = (bf16[10,4096]{1,0:T(8,128)(2,1)S(1)}, bf16[10,4096]{1,0:T(8,128)(2,1)S(1)}, u32[]{:S(2)}, u32[]{:S(2)}) collective-permute-start(bf16[10,4096]{1,0:T(8,128)(2,1)S(1)} %multiply_convert_fusion), channel_id=1, source_target_pairs={{0,8},{4,12},{8,0},{12,4},{1,9},{5,13},{9,1},{13,5},{2,10},{6,14},... | collective-permute-start | bytes 245768 | tf_op jit(solution)/shard_map/ppermute | solution.py:17
where the time goes:
time: 153 us; the launch traced here: 152 us
  blocking collectives  105 us (69%)
  starting transfers between devices  17.6 us (12%)
  matrix products  13.4 us (9%)
  other arithmetic  7.46 us (5%)
  local copies, waits for them, and re-layouts  4.66 us (3%)
  waiting for transfers between devices  3.48 us (2%)
    unnamed x1, blocking collectives  58.1 us
    psum x1, blocking collectives, on_device(): gram_in = lax.psum(gram_part, ('dp', 'mp'))  25.9 us
    all_gather x1, blocking collectives, on_device(): lax.all_gather(own_inputs, 'dp', axis=0, tiled=True)  19.2 us
    dot_general x1, matrix products, on_device(): lax.dot_general(rotated, rotated, (((1,), (1,)), ((), ())), preferred_ele...  9.39 us
    ppermute x4, starting transfers between devices, shifted(): return lax.ppermute(x, axis, [(i, (i + by) % size) for i in range(size)])  6.56 us
    all_to_all x1, starting transfers between devices, on_device(): lax.all_to_all(send_slots.reshape(expert_ways, CAP), 'expert', split_axis...  4.21 us
    all_to_all x1, starting transfers between devices, on_device(): lax.all_to_all(send_inputs.reshape(expert_ways, CAP, -1), 'expert', split...  3.43 us
    all_to_all x1, starting transfers between devices, on_device(): lax.all_to_all(send_grads.reshape(expert_ways, CAP, -1), 'expert', split_...  3.38 us
  transfers between devices with their start and end apart: 7, of which 2 were waited for; matrix products, arithmetic and copies ran while one was open for 11% of the time, Pallas kernels for 0%

commit v1 on v0

--- a/solution.py
+++ b/solution.py
@@ -1,6 +1,10 @@
+import functools
+
 import jax
 import jax.numpy as jnp
 from jax import lax
+from jax.experimental import pallas as pl
+from jax.experimental.pallas import tpu as pltpu
 from jax.sharding import PartitionSpec as P
 
 D = 6144
@@ -146,6 +150,394 @@
     return solve_system(system_rows, first_row)
 
 
+MESH = pl.DeviceIdType.MESH
+PAD = 8
+LANES = 128
+HALF_CHUNKS = 2
+
+
+def fused_kernel(
+    sizes,
+    act_hbm,
+    grad_hbm,
+    expert_ids,
+    example_ids,
+    example_slots,
+    basis_hbm,
+    in_eigen_hbm,
+    out_eigen_hbm,
+    out_ref,
+    act_v,
+    grad_v,
+    in_eigen,
+    out_eigen,
+    basis,
+    gathered,
+    grad_send,
+    grad_got,
+    part_send,
+    part_got,
+    kernel_send,
+    kernel_got,
+    local_sem,
+    basis_sem,
+    send_sem,
+    half_sem,
+    other_sem,
+    grad_sem,
+    part_sem,
+    kernel_sem,
+):
+    data_ways, expert_ways, tok, example_count = sizes
+    blocks = data_ways * expert_ways
+    order = example_count // blocks
+    rows = blocks * PAD
+    z, x, m = lax.axis_index("dp"), lax.axis_index("expert"), lax.axis_index("mp")
+    own = z * expert_ways + x
+    chunk = gathered.shape[3]
+    quarter = out_eigen.shape[1]
+    chunks = gathered.shape[0]
+
+    def at(zz, xx, mm):
+        return {"dp": zz, "expert": xx, "mp": mm}
+
+    def turn(i, by, size):
+        return lax.rem(i + by, size)
+
+    z_turns = sorted(range(1, data_ways), key=lambda d: (min(d, data_ways - d), d))
+    x_turns = range(1, expert_ways)
+    other = 1 - m
+
+    barrier = pltpu.get_barrier_semaphore()
+    peers = 0
+    for dz in range(data_ways):
+        for dx in range(expert_ways):
+            for dm in range(2):
+                if dz or dx or dm:
+                    pl.semaphore_signal(
+                        barrier,
+                        inc=1,
+                        device_id=at(
+                            turn(z, dz, data_ways), turn(x, dx, expert_ways), turn(m, dm, 2)
+                        ),
+                        device_id_type=MESH,
+                    )
+                    peers += 1
+
+    act_copy = pltpu.make_async_copy(act_hbm, act_v, local_sem.at[0])
+    act_copy.start()
+    grad_copy = pltpu.make_async_copy(grad_hbm, grad_v, local_sem.at[1])
+    grad_copy.start()
+    chunk_order = [
+        m * HALF_CHUNKS + i for i in range(HALF_CHUNKS)
+    ] + [other * HALF_CHUNKS + i for i in range(HALF_CHUNKS)]
+    basis_copies = []
+    for i, c in enumerate(chunk_order):
+        span = pl.ds(pl.multiple_of(c * chunk, chunk), chunk)
+        copy = pltpu.make_async_copy(
+            basis_hbm.at[0, span, :], basis.at[span, :], basis_sem.at[i]
+        )
+        copy.start()
+        basis_copies.append(copy)
+    in_copy = pltpu.make_async_copy(in_eigen_hbm, in_eigen, local_sem.at[2])
+    in_copy.start()
+    out_copy = pltpu.make_async_copy(
+        out_eigen_hbm.at[:, pl.ds(pl.multiple_of(z * quarter, quarter), quarter)],
+        out_eigen,
+        local_sem.at[3],
+    )
+    out_copy.start()
+
+    def padded(value):
+        value = value.astype(jnp.float32)
+        fill = jnp.zeros((PAD - tok, value.shape[1]), jnp.float32)
+        return jnp.concatenate([value, fill], axis=0).astype(jnp.bfloat16)
+
+    act_copy.wait()
+    for c in range(chunks):
+        gathered[c, own] = padded(act_v[:, c * chunk : (c + 1) * chunk])
+
+    sends = []
+
+    def send(source, target, sem, device):
+        copy = pltpu.make_async_remote_copy(
+            src_ref=source,
+            dst_ref=target,
+            send_sem=send_sem.at[len(sends)],
+            recv_sem=sem,
+            device_id=device,
+            device_id_type=MESH,
+        )
+        copy.start()
+        sends.append(copy)
+
+    def arrived(target, sem):
+        pltpu.make_async_copy(target, target, sem).wait()
+
+    pl.semaphore_wait(barrier, peers)
+
+    for i in range(HALF_CHUNKS):
+        block = gathered.at[m * HALF_CHUNKS + i, own]
+        for dx in x_turns:
+            send(block, block, half_sem.at[i, own], at(z, turn(x, dx, expert_ways), m))
+        for dz in reversed(z_turns):
+            send(block, block, half_sem.at[i, own], at(turn(z, dz, data_ways), x, m))
+
+    row_at = lax.broadcasted_iota(jnp.int32, (PAD, LANES), 0)
+    lane_at = lax.broadcasted_iota(jnp.int32, (PAD, LANES), 1)
+    table = jnp.zeros((PAD, LANES), jnp.float32)
+    for r in range(tok):
+        place = example_slots[example_ids[r]]
+        expert = expert_ids[r, 0]
+        spread = LANES // 2 + place // order * PAD + place % order
+        hit = (
+            (lane_at == place) | (lane_at == example_count + expert) | (lane_at == spread)
+        ) & (row_at == r)
+        table = jnp.where(hit, 1.0, table)
+    table = table.astype(jnp.bfloat16)
+    grad_copy.wait()
+    for q in range(data_ways):
+        grad_send[q, :, :quarter] = padded(grad_v[:, q * quarter : (q + 1) * quarter])
+        grad_send[q, :, quarter:] = table
+    grad_got[own] = grad_send[z]
+    for dz in [0] + z_turns:
+        for dx in range(expert_ways):
+            if dz or dx:
+                zz = turn(z, dz, data_ways)
+                send(
+                    grad_send.at[zz],
+                    grad_got.at[own],
+                    grad_sem.at[own],
+                    at(zz, turn(x, dx, expert_ways), m),
+                )
+
+    for i in range(HALF_CHUNKS):
+        c = m * HALF_CHUNKS + i
+        for dz in z_turns:
+            b = turn(z, dz, data_ways) * expert_ways + x
+            block = gathered.at[c, b]
+            arrived(block, half_sem.at[i, b])
+            for dx in x_turns:
+                send(block, block, half_sem.at[i, b], at(z, turn(x, dx, expert_ways), m))
+            send(block, block, other_sem.at[i, b], at(z, x, other))
+        for dz in [0] + z_turns:
+            for dx in x_turns:
+                b = turn(z, dz, data_ways) * expert_ways + turn(x, dx, expert_ways)
+                block = gathered.at[c, b]
+                arrived(block, half_sem.at[i, b])
+                send(block, block, other_sem.at[i, b], at(z, x, other))
+
+    total = jnp.zeros((rows, basis.shape[1]), jnp.float32)
+    for i, c in enumerate(chunk_order):
+        if i >= HALF_CHUNKS:
+            for dz in range(data_ways):
+                for dx in range(expert_ways):
+                    if dz or dx:
+                        b = turn(z, dz, data_ways) * expert_ways + turn(x, dx, expert_ways)
+                        arrived(gathered.at[c, b], other_sem.at[i - HALF_CHUNKS, b])
+        basis_copies[i].wait()
+        left = jnp.concatenate(
+            [gathered[c, b].astype(jnp.float32) for b in range(blocks)], axis=0
+        ).astype(jnp.bfloat16)
+        span = pl.ds(pl.multiple_of(c * chunk, chunk), chunk)
+        total = total + jnp.dot(left, basis[span, :], preferred_element_type=jnp.float32)
+
+    def gram(value):
+        return lax.dot_general(
+            value, value, (((1,), (1,)), ((), ())), preferred_element_type=jnp.float32
+        )
+
+    in_copy.wait()
+    rotated = (total * lax.rsqrt(in_eigen[...] + eigen_floor)).astype(jnp.bfloat16)
+    gram_in = gram(rotated) / D
+
+    for dz in range(data_ways):
+        for dx in range(expert_ways):
+            if dz or dx:
+                b = turn(z, dz, data_ways) * expert_ways + turn(x, dx, expert_ways)
+                arrived(grad_got.at[b], grad_sem.at[b])
+    out_copy.wait()
+    grads = jnp.concatenate(
+        [grad_got[b, :, :quarter].astype(jnp.float32) for b in range(blocks)], axis=0
+    )
+    scaled = (grads * lax.rsqrt(out_eigen[...] + eigen_floor)).astype(jnp.bfloat16)
+    gram_out = gram(scaled) / FF
+
+    part_send[...] = jnp.concatenate([gram_in, gram_out], axis=1).reshape(blocks, PAD, LANES)
+    mine = z * 2 + m
+    for dz in [0] + z_turns:
+        for dm in range(2):
+            if dz or dm:
+                zz, mm = turn(z, dz, data_ways), turn(m, dm, 2)
+                send(
+                    part_send.at[zz * 2 + mm],
+                    part_got.at[mine],
+                    part_sem.at[mine],
+                    at(zz, x, mm),
+                )
+    tables = jnp.concatenate(
+        [grad_got[b, :, quarter:].astype(jnp.float32) for b in range(blocks)], axis=0
+    )
+
+    def members(value):
+        lanes = lax.broadcasted_iota(jnp.int32, value.shape, 1)
+        chosen = jnp.where(lanes == example_count + x, value, 0.0)
+        return value * jnp.sum(chosen, axis=1, keepdims=True)
+
+    every_member = members(tables)
+    own_member = members(grad_got[mine, :, quarter:].astype(jnp.float32))
+    sums = part_send[mine]
+    for dz in range(data_ways):
+        for dm in range(2):
+            if dz or dm:
+                b = turn(z, dz, data_ways) * 2 + turn(m, dm, 2)
+                arrived(part_got.at[b], part_sem.at[b])
+                sums = sums + part_got[b]
+    weights = sums[:, :rows] * sums[:, rows:]
+    right = jnp.dot(
+        weights,
+        every_member,
+        precision=lax.Precision.HIGHEST,
+        preferred_element_type=jnp.float32,
+    )
+    pairs = lax.dot_general(
+        own_member,
+        right,
+        (((0,), (0,)), ((), ())),
+        precision=lax.Precision.HIGHEST,
+        preferred_element_type=jnp.float32,
+    )
+    kernel_send[...] = pairs[LANES // 2 :].reshape(blocks, PAD, LANES)
+    place = own * 2 + m
+    for dz in [0] + z_turns:
+        for dx in range(expert_ways):
+            for dm in range(2):
+                if dz or dx or dm:
+                    zz, xx, mm = turn(z, dz, data_ways), turn(x, dx, expert_ways), turn(m, dm, 2)
+                    send(
+                        kernel_send.at[zz * expert_ways + xx],
+                        kernel_got.at[place],
+                        kernel_sem.at[place],
+                        at(zz, xx, mm),
+                    )
+    kernel_got[place] = kernel_send[own]
+    for dz in range(data_ways):
+        for dx in range(expert_ways):
+            for dm in range(2):
+                if dz or dx or dm:
+                    zz, xx, mm = turn(z, dz, data_ways), turn(x, dx, expert_ways), turn(m, dm, 2)
+                    b = (zz * expert_ways + xx) * 2 + mm
+                    arrived(kernel_got.at[b], kernel_sem.at[b])
+    system = kernel_got[0]
+    for b in range(1, blocks * 2):
+        system = system + kernel_got[b]
+
+    work = system
+    for k in range(order):
+        column = jnp.sum(jnp.where(lane_at == own * order + k, system, 0.0), axis=1, keepdims=True)
+        column = column + jnp.where(row_at == k, ridge_term, 0.0)
+        work = jnp.where(lane_at == LANES // 2 + k, column, work)
+    for k in range(order):
+        column = jnp.sum(jnp.where(lane_at == LANES // 2 + k, work, 0.0), axis=1, keepdims=True)
+        pivot_row = work[k : k + 1, :] / column[k : k + 1, :]
+        work = jnp.where(row_at == k, pivot_row, work - column * pivot_row)
+    out_ref[...] = work[:order, :example_count]
+    for copy in sends:
+        copy.wait_send()
+
+
+def fused(
+    activations,
+    gradients,
+    expert_ids,
+    example_ids,
+    example_slots,
+    eigenbasis,
+    input_eigen,
+    output_eigen,
+):
+    data_ways = lax.axis_size("dp")
+    expert_ways = lax.axis_size("expert")
+    tok = activations.shape[0]
+    example_count = example_slots.shape[0]
+    blocks = data_ways * expert_ways
+    depth, width = eigenbasis.shape[1:]
+    chunks = 2 * HALF_CHUNKS
+    chunk = depth // chunks
+    quarter = gradients.shape[1] // data_ways
+    z_sends, x_sends = data_ways - 1, expert_ways - 1
+    send_count = (
+        HALF_CHUNKS * (z_sends + x_sends + z_sends * (x_sends + 1) + data_ways * x_sends)
+        + (blocks - 1)
+        + (data_ways * 2 - 1)
+        + (blocks * 2 - 1)
+    )
+    dma = pltpu.SemaphoreType.DMA
+    anywhere = pl.BlockSpec(memory_space=pl.ANY)
+    scalars = pl.BlockSpec(memory_space=pltpu.SMEM)
+    return pl.pallas_call(
+        functools.partial(fused_kernel, (data_ways, expert_ways, tok, example_count)),
+        out_shape=jax.ShapeDtypeStruct((example_count // blocks, example_count), jnp.float32),
+        in_specs=[anywhere, anywhere, scalars, scalars, scalars, anywhere, anywhere, anywhere],
+        out_specs=pl.BlockSpec(memory_space=pltpu.VMEM),
+        scratch_shapes=[
+            pltpu.VMEM(activations.shape, jnp.bfloat16),
+            pltpu.VMEM(gradients.shape, jnp.bfloat16),
+            pltpu.VMEM(input_eigen.shape, jnp.float32),
+            pltpu.VMEM((1, quarter), jnp.float32),
+            pltpu.VMEM((depth, width), jnp.bfloat16),
+            pltpu.VMEM((chunks, blocks, PAD, chunk), jnp.bfloat16),
+            pltpu.VMEM((data_ways, PAD, quarter + LANES), jnp.bfloat16),
+            pltpu.VMEM((blocks, PAD, quarter + LANES), jnp.bfloat16),
+            pltpu.VMEM((blocks, PAD, LANES), jnp.float32),
+            pltpu.VMEM((blocks, PAD, LANES), jnp.float32),
+            pltpu.VMEM((blocks, PAD, LANES), jnp.float32),
+            pltpu.VMEM((blocks * 2, PAD, LANES), jnp.float32),
+            dma((4,)),
+            dma((chunks,)),
+            dma((send_count,)),
+            dma((HALF_CHUNKS, blocks)),
+            dma((HALF_CHUNKS, blocks)),
+            dma((blocks,)),
+            dma((blocks,)),
+            dma((blocks * 2,)),
+        ],
+        compiler_params=pltpu.CompilerParams(
+            collective_id=0, has_side_effects=True, vmem_limit_bytes=48 * 1024 * 1024
+        ),
+    )(
+        activations,
+        gradients,
+        expert_ids,
+        example_ids,
+        example_slots,
+        eigenbasis,
+        input_eigen,
+        output_eigen,
+    )
+
+
+def fits_fused(mesh, tok, example_count):
+    data_ways, expert_ways = mesh.shape["dp"], mesh.shape["expert"]
+    blocks = data_ways * expert_ways
+    order = example_count // blocks
+    return (
+        mesh.shape["mp"] == 2
+        and data_ways * 2 == blocks
+        and blocks * PAD * 2 == LANES
+        and tok <= PAD
+        and order <= PAD
+        and example_count + expert_ways <= LANES // 2
+    )
+
+
+def on_any_slice(mesh, activations, gradients, expert_ids, example_ids, example_slots, *factors):
+    use = fits_fused(mesh, activations.shape[0], example_slots.shape[0])
+    return (fused if use else on_device)(
+        activations, gradients, expert_ids, example_ids, example_slots, *factors
+    )
+
+
 def solution(mesh):
     placed = (
         P(("groups", "dp", "expert"), None),
@@ -158,7 +550,7 @@
         P("expert", "mp"),
     )
     return jax.shard_map(
-        on_device,
+        functools.partial(on_any_slice, mesh),
         mesh=mesh,
         in_specs=placed,
         out_specs=P(("groups", "dp", "expert"), None),

time: 153 us -> 36.7 us (0.24)
  blocking collectives: 105 us -> 0 us
  Pallas kernels: 0 us -> 30.6 us
  starting transfers between devices: 17.6 us -> 0 us
  matrix products: 13.4 us -> 0 us
  other arithmetic: 7.46 us -> 0 us
  waiting for transfers between devices: 3.48 us -> 0 us
    unnamed x1 -> x0, blocking collectives: 58.1 us -> none
    pallas_call x0 -> x1, Pallas kernels: none -> 30.6 us  [fused(): pl.pallas_call(functools.partial(fused_kernel, (data_ways, expert_ways, t...]
    psum x1 -> x0, blocking collectives: 25.9 us -> none  [on_device(): gram_in = lax.psum(gram_part, ('dp', 'mp'))]
    all_gather x2 -> x0, blocking collectives: 21 us -> none  [the longest x1 19.2 us: on_device(): lax.all_gather(own_inputs, 'dp', axis=0, tiled=True)]
    dot_general x11 -> x0, matrix products: 12.5 us -> none  [the longest x1 9.39 us: on_device(): lax.dot_general(rotated, rotated, (((1,), (1,)), ((), ())), preferred_ele...]
    all_to_all x3 -> x0, starting transfers between devices: 11 us -> none  [the longest x1 4.21 us: on_device(): lax.all_to_all(send_slots.reshape(expert_ways, CAP), 'expert', split_axis...]
    ppermute x4 -> x0, starting transfers between devices: 6.56 us -> none  [shifted(): return lax.ppermute(x, axis, [(i, (i + by) % size) for i in range(size)])]
    unnamed x7 -> x14, local copies, waits for them, and re-layouts: 1.59 us -> 5.76 us
  transfers between devices with their start and end apart: 7 -> 0, of which waited for: 2 -> 0; matrix products, arithmetic and copies ran while one was open for 11% -> 0% of each run, Pallas kernels for 0% -> 0%
where the time goes in v1:
time: 36.7 us; the launch traced here: 36.4 us
  Pallas kernels  30.6 us (83%)
  local copies, waits for them, and re-layouts  5.76 us (16%)
    pallas_call x1, Pallas kernels, fused(): pl.pallas_call(functools.partial(fused_kernel, (data_ways, expert_ways, t...  30.6 us
    unnamed x14, local copies, waits for them, and re-layouts  5.76 us

profile of v1, /device:TPU:0, one launch (start us, length us, event | category | flops | bytes accessed | tf_op | source)
XLA Modules:
  0.0 36.4 jit_solution(6941991124511712979)
XLA Ops:
  0.0 0.7 %copy.9.expert_ids = s32[6,1]{1,0:T(8,128)S(1)} copy(s32[6,1]{0,1:T(1,128)} %param.10) | data formatting | bytes 48 | tf_op args[2]
  0.7 0.0 copy-start
  0.7 0.9 %copy-done = bf16[6,6144]{1,0:T(8,128)(2,1)S(1)} copy-done((bf16[6,6144]{1,0:T(8,128)(2,1)S(1)}, bf16[6,6144]{1,0:T(8,128)(2,1)}, u32[]{:S(2)}) %copy-start) | copy-done | bytes 73752
  1.6 0.0 copy-start.1
  1.6 0.8 %copy-done.1 = bf16[6,4096]{1,0:T(8,128)(2,1)S(1)} copy-done((bf16[6,4096]{1,0:T(8,128)(2,1)S(1)}, bf16[6,4096]{1,0:T(8,128)(2,1)}, u32[]{:S(2)}) %copy-start.1) | copy-done | bytes 49176
  2.5 0.0 copy-start.2
  2.5 0.7 %copy-done.2 = f32[1,4096]{1,0:T(1,128)S(1)} copy-done((f32[1,4096]{1,0:T(1,128)S(1)}, f32[1,4096]{1,0:T(1,128)}, u32[]{:S(2)}) %copy-start.2) | copy-done | bytes 16408
  3.2 0.0 copy-start.3
  3.2 0.7 %copy-done.3 = f32[1,768]{1,0:T(1,128)S(1)} copy-done((f32[1,768]{1,0:T(1,128)S(1)}, f32[1,768]{1,0:T(1,128)}, u32[]{:S(2)}) %copy-start.3) | copy-done | bytes 3096
  3.9 0.0 copy-start.4
  3.9 0.7 %copy-done.4 = s32[6]{0:T(128)S(1)} copy-done((s32[6]{0:T(128)S(1)}, s32[6]{0:T(128)}, u32[]{:S(2)}) %copy-start.4) | copy-done | bytes 48
  4.5 0.0 copy-start.5
  4.5 0.7 %copy-done.5 = s32[32]{0:T(128)S(1)} copy-done((s32[32]{0:T(128)S(1)}, s32[32]{0:T(128)}, u32[]{:S(2)}) %copy-start.5) | copy-done | bytes 152
  5.2 30.6 %shard_map.82 = f32[4,32]{1,0:T(4,128)S(1)} custom-call(bf16[6,6144]{1,0:T(8,128)(2,1)S(1)} %copy-done, bf16[6,4096]{1,0:T(8,128)(2,1)S(1)} %copy-done.1, s32[6,1]{1,0:T(8,128)S(1)} %copy.9.expert_ids, s32[6]{0:T(128)S(1)} %copy-done.4, s32[32]{0:T(128)S(1)} %copy-done.5, bf16[1,6144,768]{2,1,0:T(8,128)(2,1)} %basis_hbm.1, f32[1,768]{1,0:T(1,128)S(1)} %copy-done.3, ...), custom_call_target="tpu_custom_call" | custom-call | tf_op jit(solution)/shard_map/pallas_call | solution.py:478
  35.8 0.6 %copy.11 = f32[4,32]{1,0:T(4,128)} copy(f32[4,32]{1,0:T(4,128)S(1)} %shard_map.82) | data formatting | bytes 1024
Async XLA Ops:
  0.7 0.9 %copy-start = (bf16[6,6144]{1,0:T(8,128)(2,1)S(1)}, bf16[6,6144]{1,0:T(8,128)(2,1)}, u32[]{:S(2)}) copy-start(bf16[6,6144]{1,0:T(8,128)(2,1)} %act_hbm.1) | copy-start | bytes 221188
  1.6 0.8 %copy-start.1 = (bf16[6,4096]{1,0:T(8,128)(2,1)S(1)}, bf16[6,4096]{1,0:T(8,128)(2,1)}, u32[]{:S(2)}) copy-start(bf16[6,4096]{1,0:T(8,128)(2,1)} %grad_hbm.1) | copy-start | bytes 147460
  2.5 0.7 %copy-start.2 = (f32[1,4096]{1,0:T(1,128)S(1)}, f32[1,4096]{1,0:T(1,128)}, u32[]{:S(2)}) copy-start(f32[1,4096]{1,0:T(1,128)} %out_eigen_hbm.1) | copy-start | bytes 49156
  3.2 0.7 %copy-start.3 = (f32[1,768]{1,0:T(1,128)S(1)}, f32[1,768]{1,0:T(1,128)}, u32[]{:S(2)}) copy-start(f32[1,768]{1,0:T(1,128)} %in_eigen_hbm.1) | copy-start | bytes 9220
  3.9 0.7 %copy-start.4 = (s32[6]{0:T(128)S(1)}, s32[6]{0:T(128)}, u32[]{:S(2)}) copy-start(s32[6]{0:T(128)} %example_ids.1) | copy-start | bytes 76
  4.5 0.7 %copy-start.5 = (s32[32]{0:T(128)S(1)}, s32[32]{0:T(128)}, u32[]{:S(2)}) copy-start(s32[32]{0:T(128)} %example_slots.1) | copy-start | bytes 388

commit v2 on v1

--- a/solution.py
+++ b/solution.py
@@ -153,20 +153,25 @@
 MESH = pl.DeviceIdType.MESH
 PAD = 8
 LANES = 128
-HALF_CHUNKS = 2
+HALF_CHUNKS = 1
+ACT_GROUPS = 2 * HALF_CHUNKS
+GRAD, PART, KERNEL = ACT_GROUPS, ACT_GROUPS + 1, ACT_GROUPS + 2
 
 
 def fused_kernel(
     sizes,
     act_hbm,
     grad_hbm,
-    expert_ids,
-    example_ids,
-    example_slots,
+    expert_ids_hbm,
+    example_ids_hbm,
+    example_slots_hbm,
     basis_hbm,
     in_eigen_hbm,
     out_eigen_hbm,
     out_ref,
+    expert_ids,
+    example_ids,
+    example_slots,
     act_v,
     grad_v,
     in_eigen,
@@ -226,6 +231,18 @@
 
     act_copy = pltpu.make_async_copy(act_hbm, act_v, local_sem.at[0])
     act_copy.start()
+    id_copies = [
+        pltpu.make_async_copy(source, target, local_sem.at[4 + i])
+        for i, (source, target) in enumerate(
+            (
+                (expert_ids_hbm, expert_ids),
+                (example_ids_hbm, example_ids),
+                (example_slots_hbm, example_slots),
+            )
+        )
+    ]
+    for copy in id_copies:
+        copy.start()
     grad_copy = pltpu.make_async_copy(grad_hbm, grad_v, local_sem.at[1])
     grad_copy.start()
     chunk_order = [
@@ -257,19 +274,20 @@
     for c in range(chunks):
         gathered[c, own] = padded(act_v[:, c * chunk : (c + 1) * chunk])
 
-    sends = []
-
-    def send(source, target, sem, device):
-        copy = pltpu.make_async_remote_copy(
+    act_sends = []
+
+    def send(source, target, sem, device, group=None):
+        if group is None:
+            group = len(act_sends) // (blocks - 1)
+            act_sends.append(group)
+        pltpu.make_async_remote_copy(
             src_ref=source,
             dst_ref=target,
-            send_sem=send_sem.at[len(sends)],
+            send_sem=send_sem.at[group],
             recv_sem=sem,
             device_id=device,
             device_id_type=MESH,
-        )
-        copy.start()
-        sends.append(copy)
+        ).start()
 
     def arrived(target, sem):
         pltpu.make_async_copy(target, target, sem).wait()
@@ -286,9 +304,11 @@
     row_at = lax.broadcasted_iota(jnp.int32, (PAD, LANES), 0)
     lane_at = lax.broadcasted_iota(jnp.int32, (PAD, LANES), 1)
     table = jnp.zeros((PAD, LANES), jnp.float32)
+    for copy in id_copies:
+        copy.wait()
     for r in range(tok):
         place = example_slots[example_ids[r]]
-        expert = expert_ids[r, 0]
+        expert = expert_ids[0, r]
         spread = LANES // 2 + place // order * PAD + place % order
         hit = (
             (lane_at == place) | (lane_at == example_count + expert) | (lane_at == spread)
@@ -307,8 +327,9 @@
                 send(
                     grad_send.at[zz],
                     grad_got.at[own],
-                    grad_sem.at[own],
+                    grad_sem.at[0],
                     at(zz, turn(x, dx, expert_ways), m),
+                    group=GRAD,
                 )
 
     for i in range(HALF_CHUNKS):
@@ -319,22 +340,18 @@
             arrived(block, half_sem.at[i, b])
             for dx in x_turns:
                 send(block, block, half_sem.at[i, b], at(z, turn(x, dx, expert_ways), m))
-            send(block, block, other_sem.at[i, b], at(z, x, other))
+            send(block, block, other_sem.at[i], at(z, x, other))
         for dz in [0] + z_turns:
             for dx in x_turns:
                 b = turn(z, dz, data_ways) * expert_ways + turn(x, dx, expert_ways)
                 block = gathered.at[c, b]
                 arrived(block, half_sem.at[i, b])
-                send(block, block, other_sem.at[i, b], at(z, x, other))
+                send(block, block, other_sem.at[i], at(z, x, other))
 
     total = jnp.zeros((rows, basis.shape[1]), jnp.float32)
     for i, c in enumerate(chunk_order):
         if i >= HALF_CHUNKS:
-            for dz in range(data_ways):
-                for dx in range(expert_ways):
-                    if dz or dx:
-                        b = turn(z, dz, data_ways) * expert_ways + turn(x, dx, expert_ways)
-                        arrived(gathered.at[c, b], other_sem.at[i - HALF_CHUNKS, b])
+            arrived(gathered.at[c, pl.ds(0, blocks - 1)], other_sem.at[i - HALF_CHUNKS])
         basis_copies[i].wait()
         left = jnp.concatenate(
             [gathered[c, b].astype(jnp.float32) for b in range(blocks)], axis=0
@@ -351,11 +368,7 @@
     rotated = (total * lax.rsqrt(in_eigen[...] + eigen_floor)).astype(jnp.bfloat16)
     gram_in = gram(rotated) / D
 
-    for dz in range(data_ways):
-        for dx in range(expert_ways):
-            if dz or dx:
-                b = turn(z, dz, data_ways) * expert_ways + turn(x, dx, expert_ways)
-                arrived(grad_got.at[b], grad_sem.at[b])
+    arrived(grad_got.at[pl.ds(0, blocks - 1)], grad_sem.at[0])
     out_copy.wait()
     grads = jnp.concatenate(
         [grad_got[b, :, :quarter].astype(jnp.float32) for b in range(blocks)], axis=0
@@ -372,8 +385,9 @@
                 send(
                     part_send.at[zz * 2 + mm],
                     part_got.at[mine],
-                    part_sem.at[mine],
+                    part_sem.at[0],
                     at(zz, x, mm),
+                    group=PART,
                 )
     tables = jnp.concatenate(
         [grad_got[b, :, quarter:].astype(jnp.float32) for b in range(blocks)], axis=0
@@ -386,13 +400,9 @@
 
     every_member = members(tables)
     own_member = members(grad_got[mine, :, quarter:].astype(jnp.float32))
-    sums = part_send[mine]
-    for dz in range(data_ways):
-        for dm in range(2):
-            if dz or dm:
-                b = turn(z, dz, data_ways) * 2 + turn(m, dm, 2)
-                arrived(part_got.at[b], part_sem.at[b])
-                sums = sums + part_got[b]
+    part_got[mine] = part_send[mine]
+    arrived(part_got.at[pl.ds(0, blocks - 1)], part_sem.at[0])
+    sums = jnp.sum(part_got[...], axis=0)
     weights = sums[:, :rows] * sums[:, rows:]
     right = jnp.dot(
         weights,
@@ -417,20 +427,13 @@
                     send(
                         kernel_send.at[zz * expert_ways + xx],
                         kernel_got.at[place],
-                        kernel_sem.at[place],
+                        kernel_sem.at[0],
                         at(zz, xx, mm),
+                        group=KERNEL,
                     )
     kernel_got[place] = kernel_send[own]
-    for dz in range(data_ways):
-        for dx in range(expert_ways):
-            for dm in range(2):
-                if dz or dx or dm:
-                    zz, xx, mm = turn(z, dz, data_ways), turn(x, dx, expert_ways), turn(m, dm, 2)
-                    b = (zz * expert_ways + xx) * 2 + mm
-                    arrived(kernel_got.at[b], kernel_sem.at[b])
-    system = kernel_got[0]
-    for b in range(1, blocks * 2):
-        system = system + kernel_got[b]
+    arrived(kernel_got.at[pl.ds(0, blocks * 2 - 1)], kernel_sem.at[0])
+    system = jnp.sum(kernel_got[...], axis=0)
 
     work = system
     for k in range(order):
@@ -442,8 +445,11 @@
         pivot_row = work[k : k + 1, :] / column[k : k + 1, :]
         work = jnp.where(row_at == k, pivot_row, work - column * pivot_row)
     out_ref[...] = work[:order, :example_count]
-    for copy in sends:
-        copy.wait_send()
+    for group in range(ACT_GROUPS):
+        arrived(gathered.at[0, pl.ds(0, blocks - 1)], send_sem.at[group])
+    arrived(grad_got.at[pl.ds(0, blocks - 1)], send_sem.at[GRAD])
+    arrived(part_got.at[pl.ds(0, blocks - 1)], send_sem.at[PART])
+    arrived(kernel_got.at[pl.ds(0, blocks * 2 - 1)], send_sem.at[KERNEL])
 
 
 def fused(
@@ -465,22 +471,17 @@
     chunks = 2 * HALF_CHUNKS
     chunk = depth // chunks
     quarter = gradients.shape[1] // data_ways
-    z_sends, x_sends = data_ways - 1, expert_ways - 1
-    send_count = (
-        HALF_CHUNKS * (z_sends + x_sends + z_sends * (x_sends + 1) + data_ways * x_sends)
-        + (blocks - 1)
-        + (data_ways * 2 - 1)
-        + (blocks * 2 - 1)
-    )
     dma = pltpu.SemaphoreType.DMA
-    anywhere = pl.BlockSpec(memory_space=pl.ANY)
-    scalars = pl.BlockSpec(memory_space=pltpu.SMEM)
+    far = pl.BlockSpec(memory_space=pltpu.HBM)
     return pl.pallas_call(
         functools.partial(fused_kernel, (data_ways, expert_ways, tok, example_count)),
         out_shape=jax.ShapeDtypeStruct((example_count // blocks, example_count), jnp.float32),
-        in_specs=[anywhere, anywhere, scalars, scalars, scalars, anywhere, anywhere, anywhere],
+        in_specs=[far] * 8,
         out_specs=pl.BlockSpec(memory_space=pltpu.VMEM),
         scratch_shapes=[
+            pltpu.SMEM((1, tok), jnp.int32),
+            pltpu.SMEM((tok,), jnp.int32),
+            pltpu.SMEM((example_count,), jnp.int32),
             pltpu.VMEM(activations.shape, jnp.bfloat16),
             pltpu.VMEM(gradients.shape, jnp.bfloat16),
             pltpu.VMEM(input_eigen.shape, jnp.float32),
@@ -493,22 +494,22 @@
             pltpu.VMEM((blocks, PAD, LANES), jnp.float32),
             pltpu.VMEM((blocks, PAD, LANES), jnp.float32),
             pltpu.VMEM((blocks * 2, PAD, LANES), jnp.float32),
-            dma((4,)),
+            dma((7,)),
             dma((chunks,)),
-            dma((send_count,)),
+            dma((KERNEL + 1,)),
             dma((HALF_CHUNKS, blocks)),
-            dma((HALF_CHUNKS, blocks)),
-            dma((blocks,)),
-            dma((blocks,)),
-            dma((blocks * 2,)),
+            dma((HALF_CHUNKS,)),
+            dma((1,)),
+            dma((1,)),
+            dma((1,)),
         ],
         compiler_params=pltpu.CompilerParams(
-            collective_id=0, has_side_effects=True, vmem_limit_bytes=48 * 1024 * 1024
+            collective_id=0, has_side_effects=True, vmem_limit_bytes=60 * 1024 * 1024
         ),
     )(
         activations,
         gradients,
-        expert_ids,
+        expert_ids.T,
         example_ids,
         example_slots,
         eigenbasis,

time: 36.7 us -> 31.3 us (0.85)
  local copies, waits for them, and re-layouts: 5.76 us -> 1.26 us
  Pallas kernels: 30.6 us -> 29.8 us
    unnamed x14 -> x1, local copies, waits for them, and re-layouts: 5.76 us -> 1.26 us
    pallas_call x1, Pallas kernels: 30.6 us -> 29.8 us  [fused(): pl.pallas_call(functools.partial(fused_kernel, (data_ways, expert_ways, t...]
where the time goes in v2:
time: 31.3 us; the launch traced here: 31.1 us
  Pallas kernels  29.8 us (95%)
  local copies, waits for them, and re-layouts  1.26 us (4%)
    pallas_call x1, Pallas kernels, fused(): pl.pallas_call(functools.partial(fused_kernel, (data_ways, expert_ways, t...  29.8 us
    unnamed x1, local copies, waits for them, and re-layouts  1.26 us

profile of v2, /device:TPU:0, one launch (start us, length us, event | category | flops | bytes accessed | tf_op | source)
XLA Modules:
  0.0 31.1 jit_solution(14639306630158768382)
XLA Ops:
  0.0 29.8 %shard_map.82 = f32[4,32]{1,0:T(4,128)} custom-call(bf16[6,6144]{1,0:T(8,128)(2,1)} %act_hbm.1, bf16[6,4096]{1,0:T(8,128)(2,1)} %grad_hbm.1, s32[1,6]{1,0:T(1,128)} %bitcast.1, s32[6]{0:T(128)} %example_ids_hbm.1, s32[32]{0:T(128)} %example_slots_hbm.1, bf16[1,6144,768]{2,1,0:T(8,128)(2,1)} %basis_hbm.1, f32[1,768]{1,0:T(1,128)} %in_eigen_hbm.1, ...), custom_call_target="tpu_custom_call" | custom-call | tf_op jit(solution)/shard_map/pallas_call | solution.py:476
  29.9 1.3 %copy.10 = f32[4,32]{1,0:T(4,128)} copy(f32[4,32]{1,0:T(4,128)} %shard_map.82) | data formatting | bytes 1024

commit v3 on v2

--- a/solution.py
+++ b/solution.py
@@ -184,6 +184,7 @@
     part_got,
     kernel_send,
     kernel_got,
+    total,
     local_sem,
     basis_sem,
     send_sem,
@@ -218,7 +219,7 @@
     for dz in range(data_ways):
         for dx in range(expert_ways):
             for dm in range(2):
-                if dz or dx or dm:
+                if (dz or dx or dm) and not (dx and dm):
                     pl.semaphore_signal(
                         barrier,
                         inc=1,
@@ -348,26 +349,22 @@
                 arrived(block, half_sem.at[i, b])
                 send(block, block, other_sem.at[i], at(z, x, other))
 
-    total = jnp.zeros((rows, basis.shape[1]), jnp.float32)
-    for i, c in enumerate(chunk_order):
-        if i >= HALF_CHUNKS:
-            arrived(gathered.at[c, pl.ds(0, blocks - 1)], other_sem.at[i - HALF_CHUNKS])
-        basis_copies[i].wait()
+    def add_product(c, first):
         left = jnp.concatenate(
             [gathered[c, b].astype(jnp.float32) for b in range(blocks)], axis=0
         ).astype(jnp.bfloat16)
         span = pl.ds(pl.multiple_of(c * chunk, chunk), chunk)
-        total = total + jnp.dot(left, basis[span, :], preferred_element_type=jnp.float32)
+        product = jnp.dot(left, basis[span, :], preferred_element_type=jnp.float32)
+        total[...] = product if first else product + total[...]
 
     def gram(value):
         return lax.dot_general(
             value, value, (((1,), (1,)), ((), ())), preferred_element_type=jnp.float32
         )
 
-    in_copy.wait()
-    rotated = (total * lax.rsqrt(in_eigen[...] + eigen_floor)).astype(jnp.bfloat16)
-    gram_in = gram(rotated) / D
-
+    for i in range(HALF_CHUNKS):
+        basis_copies[i].wait()
+        add_product(chunk_order[i], i == 0)
     arrived(grad_got.at[pl.ds(0, blocks - 1)], grad_sem.at[0])
     out_copy.wait()
     grads = jnp.concatenate(
@@ -375,64 +372,79 @@
     )
     scaled = (grads * lax.rsqrt(out_eigen[...] + eigen_floor)).astype(jnp.bfloat16)
     gram_out = gram(scaled) / FF
-
-    part_send[...] = jnp.concatenate([gram_in, gram_out], axis=1).reshape(blocks, PAD, LANES)
     mine = z * 2 + m
+    tables = jnp.concatenate(
+        [grad_got[b, :, quarter:].astype(jnp.float32) for b in range(blocks)], axis=0
+    )
+
+    def members(value):
+        lanes = lax.broadcasted_iota(jnp.int32, value.shape, 1)
+        chosen = jnp.where(lanes == example_count + x, value, 0.0)
+        return value * jnp.sum(chosen, axis=1, keepdims=True)
+
+    every_member = members(tables).astype(jnp.bfloat16)
+    own_member = members(
+        jnp.concatenate(
+            [grad_got[z * 2 + i, :, quarter:].astype(jnp.float32) for i in range(2)], axis=0
+        )
+    )
+    own_member = jnp.concatenate([own_member] * 3, axis=0).astype(jnp.bfloat16)
+
+    def terms(value):
+        high = value.astype(jnp.bfloat16).astype(jnp.float32)
+        middle = (value - high).astype(jnp.bfloat16).astype(jnp.float32)
+        return jnp.concatenate([high, middle, value - high - middle], axis=0).astype(jnp.bfloat16)
+
+    for i in range(HALF_CHUNKS):
+        c = chunk_order[HALF_CHUNKS + i]
+        arrived(gathered.at[c, pl.ds(0, blocks - 1)], other_sem.at[i])
+        basis_copies[HALF_CHUNKS + i].wait()
+        add_product(c, False)
+
+    in_copy.wait()
+    rotated = (total[...] * lax.rsqrt(in_eigen[...] + eigen_floor)).astype(jnp.bfloat16)
+    gram_in = gram(rotated) / D
+
+    part_send[...] = jnp.concatenate([gram_in, gram_out], axis=1).reshape(
+        data_ways, 2 * PAD, LANES
+    )
     for dz in [0] + z_turns:
         for dm in range(2):
             if dz or dm:
                 zz, mm = turn(z, dz, data_ways), turn(m, dm, 2)
                 send(
-                    part_send.at[zz * 2 + mm],
+                    part_send.at[zz],
                     part_got.at[mine],
                     part_sem.at[0],
                     at(zz, x, mm),
                     group=PART,
                 )
-    tables = jnp.concatenate(
-        [grad_got[b, :, quarter:].astype(jnp.float32) for b in range(blocks)], axis=0
-    )
-
-    def members(value):
-        lanes = lax.broadcasted_iota(jnp.int32, value.shape, 1)
-        chosen = jnp.where(lanes == example_count + x, value, 0.0)
-        return value * jnp.sum(chosen, axis=1, keepdims=True)
-
-    every_member = members(tables)
-    own_member = members(grad_got[mine, :, quarter:].astype(jnp.float32))
-    part_got[mine] = part_send[mine]
+    part_got[mine] = part_send[z]
     arrived(part_got.at[pl.ds(0, blocks - 1)], part_sem.at[0])
     sums = jnp.sum(part_got[...], axis=0)
     weights = sums[:, :rows] * sums[:, rows:]
-    right = jnp.dot(
-        weights,
-        every_member,
-        precision=lax.Precision.HIGHEST,
-        preferred_element_type=jnp.float32,
-    )
+    right = jnp.dot(terms(weights), every_member, preferred_element_type=jnp.float32)
+    right = right[: 2 * PAD] + right[2 * PAD : 4 * PAD] + right[4 * PAD :]
     pairs = lax.dot_general(
         own_member,
-        right,
+        terms(right),
         (((0,), (0,)), ((), ())),
-        precision=lax.Precision.HIGHEST,
         preferred_element_type=jnp.float32,
     )
     kernel_send[...] = pairs[LANES // 2 :].reshape(blocks, PAD, LANES)
-    place = own * 2 + m
     for dz in [0] + z_turns:
         for dx in range(expert_ways):
-            for dm in range(2):
-                if dz or dx or dm:
-                    zz, xx, mm = turn(z, dz, data_ways), turn(x, dx, expert_ways), turn(m, dm, 2)
-                    send(
-                        kernel_send.at[zz * expert_ways + xx],
-                        kernel_got.at[place],
-                        kernel_sem.at[0],
-                        at(zz, xx, mm),
-                        group=KERNEL,
-                    )
-    kernel_got[place] = kernel_send[own]
-    arrived(kernel_got.at[pl.ds(0, blocks * 2 - 1)], kernel_sem.at[0])
+            if dz or dx:
+                zz, xx = turn(z, dz, data_ways), turn(x, dx, expert_ways)
+                send(
+                    kernel_send.at[zz * expert_ways + xx],
+                    kernel_got.at[own],
+                    kernel_sem.at[0],
+                    at(zz, xx, m),
+                    group=KERNEL,
+                )
+    kernel_got[own] = kernel_send[own]
+    arrived(kernel_got.at[pl.ds(0, blocks - 1)], kernel_sem.at[0])
     system = jnp.sum(kernel_got[...], axis=0)
 
     work = system
@@ -449,7 +461,7 @@
         arrived(gathered.at[0, pl.ds(0, blocks - 1)], send_sem.at[group])
     arrived(grad_got.at[pl.ds(0, blocks - 1)], send_sem.at[GRAD])
     arrived(part_got.at[pl.ds(0, blocks - 1)], send_sem.at[PART])
-    arrived(kernel_got.at[pl.ds(0, blocks * 2 - 1)], send_sem.at[KERNEL])
+    arrived(kernel_got.at[pl.ds(0, blocks - 1)], send_sem.at[KERNEL])
 
 
 def fused(
@@ -490,10 +502,11 @@
             pltpu.VMEM((chunks, blocks, PAD, chunk), jnp.bfloat16),
             pltpu.VMEM((data_ways, PAD, quarter + LANES), jnp.bfloat16),
             pltpu.VMEM((blocks, PAD, quarter + LANES), jnp.bfloat16),
+            pltpu.VMEM((data_ways, 2 * PAD, LANES), jnp.float32),
+            pltpu.VMEM((blocks, 2 * PAD, LANES), jnp.float32),
             pltpu.VMEM((blocks, PAD, LANES), jnp.float32),
             pltpu.VMEM((blocks, PAD, LANES), jnp.float32),
-            pltpu.VMEM((blocks, PAD, LANES), jnp.float32),
-            pltpu.VMEM((blocks * 2, PAD, LANES), jnp.float32),
+            pltpu.VMEM((blocks * PAD, width), jnp.float32),
             dma((7,)),
             dma((chunks,)),
             dma((KERNEL + 1,)),

time: 31.3 us -> 29.7 us (0.949)
  Pallas kernels: 29.8 us -> 28.3 us
    pallas_call x1, Pallas kernels: 29.8 us -> 28.3 us  [fused(): pl.pallas_call(functools.partial(fused_kernel, (data_ways, expert_ways, t...]
where the time goes in v3:
time: 29.7 us; the launch traced here: 29.6 us
  Pallas kernels  28.3 us (95%)
  local copies, waits for them, and re-layouts  1.26 us (4%)
    pallas_call x1, Pallas kernels, fused(): pl.pallas_call(functools.partial(fused_kernel, (data_ways, expert_ways, t...  28.3 us
    unnamed x1, local copies, waits for them, and re-layouts  1.26 us

profile of v3, /device:TPU:0, one launch (start us, length us, event | category | flops | bytes accessed | tf_op | source)
XLA Modules:
  0.0 29.6 jit_solution(9363264899148527674)
XLA Ops:
  0.0 28.3 %shard_map.82 = f32[4,32]{1,0:T(4,128)} custom-call(bf16[6,6144]{1,0:T(8,128)(2,1)} %act_hbm.1, bf16[6,4096]{1,0:T(8,128)(2,1)} %grad_hbm.1, s32[1,6]{1,0:T(1,128)} %bitcast.1, s32[6]{0:T(128)} %example_ids_hbm.1, s32[32]{0:T(128)} %example_slots_hbm.1, bf16[1,6144,768]{2,1,0:T(8,128)(2,1)} %basis_hbm.1, f32[1,768]{1,0:T(1,128)} %in_eigen_hbm.1, ...), custom_call_target="tpu_custom_call" | custom-call | tf_op jit(solution)/shard_map/pallas_call | solution.py:488
  28.3 1.3 %copy.10 = f32[4,32]{1,0:T(4,128)} copy(f32[4,32]{1,0:T(4,128)} %shard_map.82) | data formatting | bytes 1024

commit v4 on v3

--- a/solution.py
+++ b/solution.py
@@ -321,18 +321,6 @@
         grad_send[q, :, :quarter] = padded(grad_v[:, q * quarter : (q + 1) * quarter])
         grad_send[q, :, quarter:] = table
     grad_got[own] = grad_send[z]
-    for dz in [0] + z_turns:
-        for dx in range(expert_ways):
-            if dz or dx:
-                zz = turn(z, dz, data_ways)
-                send(
-                    grad_send.at[zz],
-                    grad_got.at[own],
-                    grad_sem.at[0],
-                    at(zz, turn(x, dx, expert_ways), m),
-                    group=GRAD,
-                )
-
     for i in range(HALF_CHUNKS):
         c = m * HALF_CHUNKS + i
         for dz in z_turns:
@@ -342,6 +330,17 @@
             for dx in x_turns:
                 send(block, block, half_sem.at[i, b], at(z, turn(x, dx, expert_ways), m))
             send(block, block, other_sem.at[i], at(z, x, other))
+        for dz in [0] + z_turns:
+            for dx in range(expert_ways):
+                if dz or dx:
+                    zz = turn(z, dz, data_ways)
+                    send(
+                        grad_send.at[zz],
+                        grad_got.at[own],
+                        grad_sem.at[0],
+                        at(zz, turn(x, dx, expert_ways), m),
+                        group=GRAD,
+                    )
         for dz in [0] + z_turns:
             for dx in x_turns:
                 b = turn(z, dz, data_ways) * expert_ways + turn(x, dx, expert_ways)

time: 29.7 us -> 29.2 us (0.983)
  Pallas kernels: 28.3 us -> 27.8 us
    pallas_call x1, Pallas kernels: 28.3 us -> 27.8 us  [fused(): pl.pallas_call(functools.partial(fused_kernel, (data_ways, expert_ways, t...]
where the time goes in v4:
time: 29.2 us; the launch traced here: 29.1 us
  Pallas kernels  27.8 us (95%)
  local copies, waits for them, and re-layouts  1.26 us (4%)
    pallas_call x1, Pallas kernels, fused(): pl.pallas_call(functools.partial(fused_kernel, (data_ways, expert_ways, t...  27.8 us
    unnamed x1, local copies, waits for them, and re-layouts  1.26 us

profile of v4, /device:TPU:0, one launch (start us, length us, event | category | flops | bytes accessed | tf_op | source)
XLA Modules:
  0.0 29.1 jit_solution(7381913289184513590)
XLA Ops:
  0.0 27.8 %shard_map.82 = f32[4,32]{1,0:T(4,128)} custom-call(bf16[6,6144]{1,0:T(8,128)(2,1)} %act_hbm.1, bf16[6,4096]{1,0:T(8,128)(2,1)} %grad_hbm.1, s32[1,6]{1,0:T(1,128)} %bitcast.1, s32[6]{0:T(128)} %example_ids_hbm.1, s32[32]{0:T(128)} %example_slots_hbm.1, bf16[1,6144,768]{2,1,0:T(8,128)(2,1)} %basis_hbm.1, f32[1,768]{1,0:T(1,128)} %in_eigen_hbm.1, ...), custom_call_target="tpu_custom_call" | custom-call | tf_op jit(solution)/shard_map/pallas_call | solution.py:487
  27.8 1.3 %copy.10 = f32[4,32]{1,0:T(4,128)} copy(f32[4,32]{1,0:T(4,128)} %shard_map.82) | data formatting | bytes 1024

commit v5 on v4

--- a/solution.py
+++ b/solution.py
@@ -293,15 +293,6 @@
     def arrived(target, sem):
         pltpu.make_async_copy(target, target, sem).wait()
 
-    pl.semaphore_wait(barrier, peers)
-
-    for i in range(HALF_CHUNKS):
-        block = gathered.at[m * HALF_CHUNKS + i, own]
-        for dx in x_turns:
-            send(block, block, half_sem.at[i, own], at(z, turn(x, dx, expert_ways), m))
-        for dz in reversed(z_turns):
-            send(block, block, half_sem.at[i, own], at(turn(z, dz, data_ways), x, m))
-
     row_at = lax.broadcasted_iota(jnp.int32, (PAD, LANES), 0)
     lane_at = lax.broadcasted_iota(jnp.int32, (PAD, LANES), 1)
     table = jnp.zeros((PAD, LANES), jnp.float32)
@@ -321,6 +312,16 @@
         grad_send[q, :, :quarter] = padded(grad_v[:, q * quarter : (q + 1) * quarter])
         grad_send[q, :, quarter:] = table
     grad_got[own] = grad_send[z]
+
+    pl.semaphore_wait(barrier, peers)
+
+    for i in range(HALF_CHUNKS):
+        block = gathered.at[m * HALF_CHUNKS + i, own]
+        for dx in x_turns:
+            send(block, block, half_sem.at[i, own], at(z, turn(x, dx, expert_ways), m))
+        for dz in z_turns:
+            send(block, block, half_sem.at[i, own], at(turn(z, dz, data_ways), x, m))
+
     for i in range(HALF_CHUNKS):
         c = m * HALF_CHUNKS + i
         for dz in z_turns:

time: 29.2 us -> 28.4 us (0.973)
  Pallas kernels: 27.8 us -> 27 us
    pallas_call x1, Pallas kernels: 27.8 us -> 27 us  [fused(): pl.pallas_call(functools.partial(fused_kernel, (data_ways, expert_ways, t...]
where the time goes in v5:
time: 28.4 us; the launch traced here: 28.3 us
  Pallas kernels  27 us (95%)
  local copies, waits for them, and re-layouts  1.26 us (4%)
    pallas_call x1, Pallas kernels, fused(): pl.pallas_call(functools.partial(fused_kernel, (data_ways, expert_ways, t...  27 us
    unnamed x1, local copies, waits for them, and re-layouts  1.26 us

profile of v5, /device:TPU:0, one launch (start us, length us, event | category | flops | bytes accessed | tf_op | source)
XLA Modules:
  0.0 28.3 jit_solution(7179617765515561082)
XLA Ops:
  0.0 27.0 %shard_map.82 = f32[4,32]{1,0:T(4,128)} custom-call(bf16[6,6144]{1,0:T(8,128)(2,1)} %act_hbm.1, bf16[6,4096]{1,0:T(8,128)(2,1)} %grad_hbm.1, s32[1,6]{1,0:T(1,128)} %bitcast.1, s32[6]{0:T(128)} %example_ids_hbm.1, s32[32]{0:T(128)} %example_slots_hbm.1, bf16[1,6144,768]{2,1,0:T(8,128)(2,1)} %basis_hbm.1, f32[1,768]{1,0:T(1,128)} %in_eigen_hbm.1, ...), custom_call_target="tpu_custom_call" | custom-call | tf_op jit(solution)/shard_map/pallas_call | solution.py:488
  27.0 1.3 %copy.10 = f32[4,32]{1,0:T(4,128)} copy(f32[4,32]{1,0:T(4,128)} %shard_map.82) | data formatting | bytes 1024
